TPU v7x, 512 devices: a whole 4x4x16 slice. The times are simulated.
512 devices in a mesh: row: 16 (over x, z_hi, core), col: 32 (over y, z_lo).
Axes of the slice: x: 4, y: 4, z: 16 (z_hi: 2, z_lo: 8; z = z_hi * 8 + z_lo), core: 2. Of those that a mesh axis runs over, the one named last changes fastest.
Arguments:
- anomalies: bfloat16 [128, 131072], P(None, ('col', 'row')), may hold values from -16 to 16
- vectors: bfloat16 [64, 131072], P(None, ('col', 'row')), may hold values from -0.1796875 to 0.1796875
Outputs:
- applied: float32 [64, 65536], P(None, ('row', 'col'))
All inputs are finite; a program needn't handle non-finite values.
Results may differ from a plain program's by a relative error of at most 0.0035.
Values may be sent and summed in bfloat16 or wider, within the bound.
A program may use at most 64 MiB of HBM per device.

v0:
```python
import math

import jax
import jax.numpy as jnp
from jax import lax
from jax.sharding import PartitionSpec as P


def from_root(value, axis, source):
    kept = jnp.where(lax.axis_index(axis) == source, value, 0).astype(value.dtype)
    return lax.psum(kept, axis)


def spreads(anomaly_block, inverse):
    wide = anomaly_block.astype(jnp.float32)
    return jnp.sqrt(jnp.sum(wide * wide, axis=0) * inverse + 1e-06)


def localize(row_part, row_spread, col_anom, col_spread, col_vec, inverse):
    cov = (
        lax.dot_general(
            row_part, col_anom, (((0,), (0,)), ((), ())), preferred_element_type=jnp.float32
        )
        * inverse
    )
    corr = cov / (row_spread[:, None] * col_spread[None, :])
    local = (corr * corr * corr * cov).astype(jnp.bfloat16)
    return lax.dot_general(
        col_vec, local, (((1,), (1,)), ((), ())), preferred_element_type=jnp.float32
    )


def per_device(anomalies, vectors):
    members = anomalies.shape[0]
    inverse = 1.0 / (members - 1.0)
    col_anom, col_vec = (
        lax.all_gather(anomalies, "row", axis=1, tiled=True),
        lax.all_gather(vectors, "row", axis=1, tiled=True),
    )
    row_anom = from_root(col_anom, "col", lax.axis_index("row"))
    tile_len = row_anom.shape[1]
    row_block = math.gcd(tile_len, 256)
    count = tile_len // row_block
    row_spread = spreads(row_anom, inverse)
    col_spread = spreads(col_anom, inverse)
    blocks = row_anom.reshape(members, count, row_block).transpose(1, 0, 2)
    spread_blocks = row_spread.reshape(count, row_block)

    def one_block(inputs_pair):
        return localize(inputs_pair[0], inputs_pair[1], col_anom, col_spread, col_vec, inverse)

    stacked = lax.map(one_block, (blocks, spread_blocks))
    partial_out = stacked.transpose(1, 0, 2).reshape(col_vec.shape[0], tile_len)
    return lax.psum_scatter(partial_out, "col", scatter_dimension=1, tiled=True)


def solution(mesh):
    return jax.shard_map(
        per_device,
        mesh=mesh,
        in_specs=(P(None, ("col", "row")), P(None, ("col", "row"))),
        out_specs=P(None, ("row", "col")),
        check_vma=False,
    )
```

profile of v0, /device:TPU:4, one launch (start us, length us, event | category | flops | bytes accessed | tf_op | source)
XLA Modules:
  0.0 838.4 jit_solution(18037310037777563038)
XLA Ops:
  6.5 0.0 all-gather.2.cloned.1.call-start
  6.5 0.7 all-gather.2.cloned.1.call-update
  7.3 0.0 all-reduce.2.cloned.1.call-start
  7.3 83.1 %all-gather.2.cloned.1.call-done = bf16[128,4096]{1,0:T(8,128)(2,1)} async-done(((bf16[128,256]{1,0:T(8,128)(2,1)}), bf16[128,4096]{1,0:T(8,128)(2,1)}) %all-gather.2.cloned.1.call-update) | async-done | bytes 1048592 | tf_op jit(solution)/shard_map/all_gather | solution.py:37
  90.4 0.0 copy-start.2
  90.4 1.1 broadcast_select_fusion
  91.5 0.0 copy-start
  91.5 0.0 all-reduce.2.cloned.1.call-update
  91.5 0.0 reduce-scatter.2.cloned.1.call-start
  91.6 0.0 copy-done.2
  91.6 48.1 %all_gather.7 = bf16[64,4096]{1,0:T(8,128)(2,1)} all-gather(bf16[64,256]{1,0:T(8,128)(2,1)S(1)} %copy-done.2), channel_id=1, replica_groups=mesh['row'=16,'col'=32] {'row'}, dimensions={1}, use_global_device_ids=true | all-gather | bytes 557056 | tf_op jit(solution)/shard_map/all_gather | solution.py:38
  139.7 0.0 copy-done
  139.7 0.2 multiply_reduce_fusion
  140.0 406.3 %all-reduce.2.cloned.1.call-done = bf16[128,4096]{1,0:T(8,128)(2,1)} async-done(((bf16[128,4096]{1,0:T(8,128)(2,1)}), bf16[128,4096]{1,0:T(8,128)(2,1)}) %all-reduce.2.cloned.1.call-update) | async-done | bytes 1048592 | tf_op jit(solution)/shard_map/psum | solution.py:11
  546.3 0.0 copy-start.1
  546.3 1.4 copy.8
  547.7 0.1 copy-done.1
  547.8 0.2 multiply_reduce_fusion.1
  548.1 42.2 %while.10 = (s32[]{:T(128)}, f32[16,64,256]{2,1,0:T(8,128)S(1)}, bf16[16,128,256]{2,1,0:T(8,128)(2,1)S(1)}, bf16[128,4096]{1,0:T(8,128)(2,1)S(1)}, f32[16,256]{1...) while((s32[]{:T(128)}, f32[16,64,256]{2,1,0:T(8,128)S(1)}, ...), condition=%wide.region_4.5_spmd, body=%wide.region_3.4_spmd.sunk | while | flops 409993216 | bytes 1724505 | solution.py:52
  548.1 2.6 fusion.21
  550.8 2.6 fusion.21
  553.4 2.6 fusion.21
  556.1 2.6 fusion.21
  558.7 2.6 fusion.21
  561.3 2.6 fusion.21
  564.0 2.6 fusion.21
  566.6 2.6 fusion.21
  569.3 2.6 fusion.21
  571.9 2.6 fusion.21
  574.5 2.6 fusion.21
  577.2 2.6 fusion.21
  579.8 2.6 fusion.21
  582.5 2.6 fusion.21
  585.1 2.6 fusion.21
  587.7 2.6 fusion.21
  590.4 1.1 copy.6
  591.4 0.0 reduce-scatter.2.cloned.1.call-update
  591.5 240.4 %reduce-scatter.2.cloned.1.call-done = f32[64,128]{1,0:T(8,128)} async-done(((f32[64,4096]{1,0:T(8,128)}), f32[64,128]{1,0:T(8,128)}) %reduce-scatter.2.cloned.1.call-update) | async-done | bytes 32784 | tf_op jit(solution)/shard_map/reduce_scatter | solution.py:54
  (20 shorter events, 0.2 us)
Async XLA Ops:
  6.5 83.9 %all-gather.2.cloned.1.call-start = ((), (), s32[]{:S(2)}) async-start(), calls=%async_computation.1 | async-start | bytes 1114112 | tf_op jit(solution)/shard_map/all_gather | solution.py:37
  7.3 539.0 %all-reduce.2.cloned.1.call-start = ((), (), s32[]{:S(2)}) async-start(), calls=%async_computation.2 | async-start | bytes 2097152 | tf_op jit(solution)/shard_map/psum | solution.py:11
  90.4 1.2 copy-start.2
  91.5 48.2 %copy-start = (bf16[128,4096]{1,0:T(8,128)(2,1)S(1)}, bf16[128,4096]{1,0:T(8,128)(2,1)}, u32[]{:S(2)}) copy-start(bf16[128,4096]{1,0:T(8,128)(2,1)} %all-gather.2.cloned.1.call-done) | copy-start | bytes 3145732
  91.5 740.3 %reduce-scatter.2.cloned.1.call-start = ((), (), s32[]{:S(2)}) async-start(), calls=%async_computation.3 | async-start | bytes 1081344 | tf_op jit(solution)/shard_map/reduce_scatter | solution.py:54
  546.3 1.5 copy-start.1
Sparse Core Ops, SparseCore 0:
  10.5 79.8 all-gather.1
  93.3 452.9 all-reduce.1
  591.6 240.2 reduce-scatter.1
where the time goes:
time: 839 us; the launch traced here: 838 us
  waiting for transfers between devices  731 us (87%)
  blocking collectives  48.1 us (6%)
  matrix products  41.6 us (5%)
  between operations  13.2 us (2%)
    psum x1, waiting for transfers between devices, from_root(): return lax.psum(kept, axis)  406 us
    reduce_scatter x1, waiting for transfers between devices, per_device(): return lax.psum_scatter(partial_out, 'col', scatter_dimension=1, tiled=True)  240 us
    all_gather x1, waiting for transfers between devices, per_device(): lax.all_gather(anomalies, 'row', axis=1, tiled=True)  83.1 us
    all_gather x1, blocking collectives, per_device(): lax.all_gather(vectors, 'row', axis=1, tiled=True)  48.1 us
    dot_general x16, matrix products, localize(): lax.dot_general(col_vec, local, (((1,), (1,)), ((), ())), preferred_eleme...  41.6 us
  transfers between devices with their start and end apart: 3, of which 3 were waited for; matrix products, arithmetic and copies ran while one was open for 0% of the time, Pallas kernels for 0%

commit v1 on v0

v1 whole, which is shorter than its diff:
```python
import jax
import jax.numpy as jnp
from jax import lax
from jax.experimental import pallas as pl
from jax.experimental.pallas import tpu as pltpu
from jax.sharding import PartitionSpec as P

MESH = pl.DeviceIdType.MESH
F32 = jnp.float32
BF16 = jnp.bfloat16
MEMBERS = 128
VECS = 64
INV = 1.0 / (MEMBERS - 1.0)
JROWS = 400
IROWS = 272

ORDER = [
    (0, 0), (1, 0), (3, 0), (0, 1), (0, 3), (2, 0), (0, 2), (1, 1),
    (1, 3), (3, 1), (3, 3), (1, 2), (3, 2), (2, 1), (2, 3), (2, 2),
]
SLOT = {off: n for n, off in enumerate(ORDER)}
EARLY = [(0, 5), (16, 5)]
LATE = [(5, 6), (11, 5), (21, 6), (27, 5)]


def dot(a, b):
    return jnp.dot(a, b, preferred_element_type=F32)


def split_three(c):
    hi = c.astype(BF16).astype(F32)
    rest = c - hi
    mid = rest.astype(BF16).astype(F32)
    return hi, mid, rest - mid


def kernel(a_ref, v_ref, o_ref, jbuf, vbuf, ibuf, imsg, acc, rsm, rsp,
           send_sem, jrecv, irecv, mrecv, precv, local_sem):
    row, col = lax.axis_index("row"), lax.axis_index("col")
    x, zh, core = row // 4, (row // 2) % 2, row % 2
    y, zl = col // 8, col % 8
    z = zh * 8 + zl

    def at(x_, y_, z_, core_):
        return {"row": x_ * 4 + (z_ // 8) * 2 + core_, "col": y_ * 8 + z_ % 8}

    p = x + core * (y - x)
    q = y + core * (x - y)

    def at_pq(p_, q_):
        return at(p_ + core * (q_ - p_), q_ + core * (p_ - q_), z, core)

    sib = at(x, y, z, 1 - core)
    p_up, p_dn = at_pq((p + 1) % 4, q), at_pq((p + 3) % 4, q)
    q_up, q_dn = at_pq(p, (q + 1) % 4), at_pq(p, (q + 3) % 4)
    z_up, z_dn = at(x, y, (z + 1) % 16, core), at(x, y, (z + 15) % 16, core)

    gives = y < 2
    sd = 4 * ((zl // 2) % 2) + 2 * zh + core
    tx, ty, tc = 2 * (y % 2) + zl // 4, x, zl % 2
    same_line = (tx == x) & (ty == y) & (tc == core) & gives
    own_lo, own_hi = same_line & (z == sd), same_line & (z == sd + 8)
    s0 = zl
    gy, gx = x // 2, y
    gzl = (x % 2) * 4 + 2 * (s0 // 4) + core
    gz = 8 * ((s0 % 4) // 2) + gzl
    gc = s0 % 2
    from_self = (gx == x) & (gy == y) & (gz == z) & (gc == core)

    barrier = pltpu.get_barrier_semaphore()
    for dev in (sib, p_up, p_dn, q_up, q_dn, z_up, z_dn):
        pl.semaphore_signal(barrier, inc=1, device_id=dev, device_id_type=MESH)

    @pl.when(jnp.logical_not(from_self))
    def _():
        pl.semaphore_signal(barrier, inc=1, device_id=at(gx, gy, gz, gc), device_id_type=MESH)

    wide = a_ref[...].astype(F32)
    spread = jnp.sqrt(jnp.sum(wide * wide, axis=0, keepdims=True) * INV + 1e-06)
    e = jnp.full_like(spread, 2.0**10)
    for k in range(-9, 5):
        e = jnp.where(spread >= 2.0**k, 2.0**-k, e)
    se = spread * e
    factor = 1.0 / (se * se * se * e)
    scaled = wide * e
    jbuf[0, 0:256, :] = scaled.T.astype(BF16)
    jbuf[0, 256:320, :] = v_ref[:, 0:128]
    jbuf[0, 320:384, :] = v_ref[:, 128:256]
    line = lax.broadcasted_iota(jnp.int32, (16, 128), 0)
    rows = jnp.zeros((16, 128), F32)
    for half in range(2):
        for n, part in enumerate(split_three(factor[:, half * 128:half * 128 + 128])):
            rows = jnp.where(line == half * 8 + n, part, rows)
    rows = rows.astype(BF16)
    jbuf[0, 384:400, :] = rows
    narrow = scaled.astype(BF16)
    imsg[0:128, :] = narrow[:, 0:128]
    imsg[128:256, :] = narrow[:, 128:256]
    imsg[256:272, :] = rows

    n_targets = jnp.where(gives, 2, 0) - jnp.where(own_lo | own_hi, 1, 0)
    pl.semaphore_wait(barrier, 7 + n_targets)

    sent = []

    def send(src, dst, recv, dev):
        copy = pltpu.make_async_remote_copy(
            src_ref=src, dst_ref=dst, send_sem=send_sem.at[len(sent)], recv_sem=recv,
            device_id=dev, device_id_type=MESH,
        )
        sent.append(copy)
        copy.start()

    def arrived(dst, recv):
        pltpu.make_async_remote_copy(
            src_ref=dst, dst_ref=dst, send_sem=send_sem.at[0], recv_sem=recv,
            device_id=sib, device_id_type=MESH,
        ).wait_recv()

    def seed(n, is_self):
        return pltpu.make_async_remote_copy(
            src_ref=imsg, dst_ref=ibuf.at[sd], send_sem=local_sem.at[n], recv_sem=irecv.at[0],
            device_id=at(tx, ty, sd + 8 * n, tc), device_id_type=MESH,
        ), gives & jnp.logical_not(is_self)

    seeds = [seed(0, own_lo), seed(1, own_hi)]
    for copy, cond in seeds:
        pl.when(cond)(copy.start)

    def jsend(src, dst, dev):
        send(jbuf.at[src], jbuf.at[dst], jrecv.at[dst], dev)

    def jwait(n):
        arrived(jbuf.at[n], jrecv.at[n])

    def to_sib(n):
        jsend(n, 16 + n, sib)

    def prep(n):
        rows = jbuf[n, 384:400, :].astype(F32)
        for half in range(2):
            f = jnp.sum(rows[half * 8:half * 8 + 8, :], axis=0, keepdims=True)
            w = jbuf[n, 256 + half * 64:320 + half * 64, :].astype(F32) * f
            hi = w.astype(BF16)
            lo = (w - hi.astype(F32)).astype(BF16)
            lanes = slice(n * 256 + half * 128, n * 256 + half * 128 + 128)
            vbuf[0:64, lanes] = hi
            vbuf[64:128, lanes] = lo

    def q_both(dp, dq):
        n = SLOT[dp, dq]
        jsend(n, SLOT[dp, (dq + 3) % 4], q_up)
        jsend(n, SLOT[dp, (dq + 1) % 4], q_dn)

    def q_across(dp):
        f = (p + q + dp) % 2
        n1, n3 = SLOT[dp, 1], SLOT[dp, 3]
        src = n1 + f * (n3 - n1)
        jsend(src, SLOT[dp, 2], at_pq(p, (q + 3 + 2 * f) % 4))

    jsend(0, SLOT[3, 0], p_up)
    jsend(0, SLOT[1, 0], p_dn)
    q_both(0, 0)
    to_sib(0)
    prep(0)

    def ichunk(s):
        return ibuf.at[s]

    def isend(k, dev, step):
        s = (z + k + 8) % 8
        send(ichunk(s), ichunk(s), irecv.at[step], dev)

    def iwait(k, step):
        s = (z + k + 8) % 8
        arrived(ichunk(s), irecv.at[step])

    def tile(groups, weights):
        total = None
        for first, n in groups:
            states = jbuf[first:first + n, 0:256, :].reshape(n * 256, 128)
            prod = dot(states, weights)
            square = prod * prod
            local = (square * square).astype(BF16)
            part = dot(vbuf[:, first * 256:(first + n) * 256], local)
            total = part if total is None else total + part
        return total[0:64, :] + total[64:128, :]

    def early_tiles(ks):
        parts, rels = [], []
        for k in ks:
            s = (z + k + 8) % 8
            for half in range(2):
                parts.append(ibuf[s, half * 128:half * 128 + 128, :])
                rels.append((2 * s + half - z + 16) % 16)
        total = tile(EARLY, jnp.concatenate(parts, axis=1))
        for n, rel in enumerate(rels):
            acc[rel] = total[:, n * 128:n * 128 + 128]

    @pl.when(from_self)
    def _():
        copy = pltpu.make_async_copy(imsg, ibuf.at[s0], local_sem.at[2])
        copy.start()
        copy.wait()

    @pl.when(jnp.logical_not(from_self))
    def _():
        arrived(ibuf.at[s0], irecv.at[0])

    isend(0, z_up, 1)
    isend(0, z_dn, 5)

    jwait(SLOT[1, 0])
    jwait(SLOT[3, 0])
    f = p % 2
    jsend(SLOT[1, 0] + f * (SLOT[3, 0] - SLOT[1, 0]), SLOT[2, 0], at_pq((p + 3 + 2 * f) % 4, q))
    q_both(1, 0)
    q_both(3, 0)
    to_sib(SLOT[1, 0])
    to_sib(SLOT[3, 0])
    jwait(SLOT[0, 1])
    jwait(SLOT[0, 3])
    q_across(0)
    to_sib(SLOT[0, 1])
    to_sib(SLOT[0, 3])
    for n in range(1, 5):
        prep(n)
    for n in range(16, 21):
        jwait(n)
        prep(n)

    early_tiles([0])
    iwait(-1, 1)
    isend(-1, z_up, 2)
    iwait(1, 5)
    isend(1, z_dn, 6)
    jwait(SLOT[2, 0])
    q_both(2, 0)
    to_sib(SLOT[2, 0])
    jwait(SLOT[0, 2])
    to_sib(SLOT[0, 2])
    early_tiles([-1, 1])
    iwait(-2, 2)
    isend(-2, z_up, 3)
    iwait(2, 6)
    isend(2, z_dn, 7)
    for dp in (1, 3):
        jwait(SLOT[dp, 1])
        jwait(SLOT[dp, 3])
        q_across(dp)
        to_sib(SLOT[dp, 1])
        to_sib(SLOT[dp, 3])
    early_tiles([-2, 2])
    iwait(-3, 3)
    isend(-3, z_up, 4)
    iwait(3, 7)
    jwait(SLOT[2, 1])
    jwait(SLOT[2, 3])
    q_across(2)
    to_sib(SLOT[2, 1])
    to_sib(SLOT[2, 3])
    for dp in (1, 3):
        jwait(SLOT[dp, 2])
        to_sib(SLOT[dp, 2])
    early_tiles([-3, 3])
    iwait(-4, 4)
    jwait(SLOT[2, 2])
    to_sib(SLOT[2, 2])
    early_tiles([-4])
    for n in list(range(5, 16)):
        prep(n)
    for n in range(21, 32):
        jwait(n)
        prep(n)

    def chunk(rel):
        d = (z + rel) % 16
        return ibuf[d // 2, pl.ds(pl.multiple_of((d % 2) * 128, 128), 128), :]

    for k in range(8):
        below, above = 8 + k, (8 - k) % 8
        total = tile(LATE, jnp.concatenate([chunk(below), chunk(above)], axis=1))
        acc[below] += total[:, 0:128]
        acc[above] += total[:, 128:256]
        if k >= 1:
            arrived(rsm.at[k - 1], mrecv.at[k - 1])
            acc[below] += rsm[k - 1]
        send(acc.at[below], rsm.at[k], mrecv.at[k], z_dn)
        if k >= 2:
            arrived(rsp.at[k - 2], precv.at[k - 2])
            acc[above] += rsp[k - 2]
        if k >= 1:
            send(acc.at[above], rsp.at[k - 1], precv.at[k - 1], z_up)

    half = z % 2
    rows = ibuf[z // 2, 256:272, :].astype(F32)
    f0 = jnp.sum(rows[0:8, :], axis=0, keepdims=True)
    f1 = jnp.sum(rows[8:16, :], axis=0, keepdims=True)
    scale = jnp.where(half == 0, f0, f1) * (INV**4)
    arrived(rsm.at[7], mrecv.at[7])
    arrived(rsp.at[6], precv.at[6])
    o_ref[...] = (acc[0] + rsm[7] + rsp[6]) * scale

    for copy in sent:
        copy.wait_send()
    for copy, cond in seeds:
        pl.when(cond)(copy.wait_send)


def per_device(anomalies, vectors):
    vmem = pl.BlockSpec(memory_space=pltpu.VMEM)
    return pl.pallas_call(
        kernel,
        out_shape=jax.ShapeDtypeStruct((VECS, 128), F32),
        in_specs=[vmem, vmem],
        out_specs=vmem,
        scratch_shapes=[
            pltpu.VMEM((32, JROWS, 128), BF16),
            pltpu.VMEM((128, 8192), BF16),
            pltpu.VMEM((8, IROWS, 128), BF16),
            pltpu.VMEM((IROWS, 128), BF16),
            pltpu.VMEM((16, VECS, 128), F32),
            pltpu.VMEM((8, VECS, 128), F32),
            pltpu.VMEM((7, VECS, 128), F32),
            pltpu.SemaphoreType.DMA((80,)),
            pltpu.SemaphoreType.DMA((32,)),
            pltpu.SemaphoreType.DMA((8,)),
            pltpu.SemaphoreType.DMA((8,)),
            pltpu.SemaphoreType.DMA((7,)),
            pltpu.SemaphoreType.DMA((3,)),
        ],
        compiler_params=pltpu.CompilerParams(
            collective_id=0, has_side_effects=True, vmem_limit_bytes=48 * 2**20
        ),
    )(anomalies, vectors)


def solution(mesh):
    return jax.shard_map(
        per_device,
        mesh=mesh,
        in_specs=(P(None, ("col", "row")), P(None, ("col", "row"))),
        out_specs=P(None, ("row", "col")),
        check_vma=False,
    )
```

time: 839 us -> 76.7 us (0.09)
  the two profiles are of different devices: /device:TPU:4 before, /device:TPU:8 now
where the time goes in v1:
time: 76.7 us; the launch traced here: 76.4 us
  Pallas kernels  74.2 us (97%)
  local copies, waits for them, and re-layouts  2.21 us (3%)
    pallas_call x1, Pallas kernels, per_device(): pl.pallas_call(kernel, out_shape=jax.ShapeDtypeStruct((VECS, 128), F32),...  74.2 us
    unnamed x5, local copies, waits for them, and re-layouts  2.21 us

profile of v1, /device:TPU:8, one launch (start us, length us, event | category | flops | bytes accessed | tf_op | source)
XLA Modules:
  0.0 76.4 jit_solution(6940455268478587738)
XLA Ops:
  0.0 0.0 copy-start
  0.0 0.8 %copy-done = bf16[128,256]{1,0:T(8,128)(2,1)S(1)} copy-done((bf16[128,256]{1,0:T(8,128)(2,1)S(1)}, bf16[128,256]{1,0:T(8,128)(2,1)}, u32[]{:S(2)}) %copy-start) | copy-done | bytes 65560
  0.8 0.0 copy-start.1
  0.8 0.8 copy-done.1
  1.6 74.2 %shard_map.28 = f32[64,128]{1,0:T(8,128)S(1)} custom-call(bf16[128,256]{1,0:T(8,128)(2,1)S(1)} %copy-done, bf16[64,256]{1,0:T(8,128)(2,1)S(1)} %copy-done.1), custom_call_target="tpu_custom_call" | custom-call | tf_op jit(solution)/shard_map/pallas_call | solution.py:312
  75.8 0.6 copy.4
Async XLA Ops:
  0.0 0.8 %copy-start = (bf16[128,256]{1,0:T(8,128)(2,1)S(1)}, bf16[128,256]{1,0:T(8,128)(2,1)}, u32[]{:S(2)}) copy-start(bf16[128,256]{1,0:T(8,128)(2,1)} %a_ref.1) | copy-start | bytes 196612
  0.8 0.8 copy-start.1

commit v2 on v0

v2 whole, which is shorter than its diff:
```python
import jax
import jax.numpy as jnp
from jax import lax
from jax.experimental import pallas as pl
from jax.experimental.pallas import tpu as pltpu
from jax.sharding import PartitionSpec as P

MESH = pl.DeviceIdType.MESH
F32 = jnp.float32
BF16 = jnp.bfloat16
MEMBERS = 128
VECS = 64
INV = 1.0 / (MEMBERS - 1.0)
JROWS = 400
IROWS = 144

ORDER = [
    (0, 0), (1, 0), (3, 0), (0, 1), (0, 3), (2, 0), (0, 2), (1, 1),
    (1, 3), (3, 1), (3, 3), (1, 2), (3, 2), (2, 1), (2, 3), (2, 2),
]
SLOT = {off: n for n, off in enumerate(ORDER)}
FIRST = [(0, 5), (16, 5)]
SECOND = [(5, 6), (21, 6)]
THIRD = [(11, 5), (27, 5)]


def dot(a, b):
    return jnp.dot(a, b, preferred_element_type=F32)


def split_three(c):
    hi = c.astype(BF16).astype(F32)
    rest = c - hi
    mid = rest.astype(BF16).astype(F32)
    return hi, mid, rest - mid


def kernel(a_ref, v_ref, o_ref, jbuf, vbuf, ibuf, imsg, acc, outbox, inbox,
           send_sem, jrecv, irecv, rrecv, misc, zsem, wsem, xsem, ysem, csem):
    row, col = lax.axis_index("row"), lax.axis_index("col")
    x, zh, core = row // 4, (row // 2) % 2, row % 2
    y, zl = col // 8, col % 8
    z = zh * 8 + zl

    def at(x_, y_, z_, core_):
        return {"row": x_ * 4 + (z_ // 8) * 2 + core_, "col": y_ * 8 + z_ % 8}

    p = x + core * (y - x)
    q = y + core * (x - y)

    def at_pq(dp, dq):
        p_, q_ = (p + dp) % 4, (q + dq) % 4
        return at(p_ + core * (q_ - p_), q_ + core * (p_ - q_), z, core)

    def at_z(d):
        return at(x, y, (z + d + 16) % 16, core)

    def signal(sem, dev):
        pl.semaphore_signal(sem, inc=1, device_id=dev, device_id_type=MESH)

    sib = at(x, y, z, 1 - core)
    mirror = at(x, 3 - y, z, core)
    half = y // 2
    source_y = y + half * (3 - 2 * y)

    barrier = pltpu.get_barrier_semaphore()
    partners = [sib] + [at_pq(d, 0) for d in (1, 2, 3)] + [at_pq(0, d) for d in (1, 2, 3)]
    partners += [at_z(d) for d in (1, -1, 2, -2, 3, -3)]
    for dev in partners:
        signal(barrier, dev)

    wide = a_ref[...].astype(F32)
    spread = jnp.sqrt(jnp.sum(wide * wide, axis=0, keepdims=True) * INV + 1e-06)
    e = jnp.full_like(spread, 2.0**10)
    for k in range(-9, 5):
        e = jnp.where(spread >= 2.0**k, 2.0**-k, e)
    se = spread * e
    factor = 1.0 / (se * se * se * e)
    scaled = wide * e
    narrow = scaled.astype(BF16)
    line = lax.broadcasted_iota(jnp.int32, (16, 128), 0)
    zero = jnp.zeros((16, 128), F32)
    halves = []
    for h in range(2):
        rows = zero
        for n, part in enumerate(split_three(factor[:, h * 128:h * 128 + 128])):
            rows = jnp.where(line == h * 8 + n, part, rows)
        halves.append(rows)

    @pl.when(y < 2)
    def _():
        ibuf[0, 0:128, :] = narrow[:, 0:128]
        ibuf[0, 128:144, :] = halves[0].astype(BF16)
        imsg[0:128, :] = narrow[:, 128:256]
        imsg[128:144, :] = halves[1].astype(BF16)

    jbuf[0, 0:256, :] = scaled.T.astype(BF16)
    jbuf[0, 256:320, :] = v_ref[:, 0:128]
    jbuf[0, 320:384, :] = v_ref[:, 128:256]
    jbuf[0, 384:400, :] = (halves[0] + halves[1]).astype(BF16)

    pl.semaphore_wait(barrier, len(partners))

    sent = []

    def remote(src, dst, recv, dev):
        copy = pltpu.make_async_remote_copy(
            src_ref=src, dst_ref=dst, send_sem=send_sem.at[len(sent)], recv_sem=recv,
            device_id=dev, device_id_type=MESH,
        )
        sent.append(copy)
        return copy

    def send(*args):
        remote(*args).start()

    def arrived(dst, recv):
        pltpu.make_async_remote_copy(
            src_ref=dst, dst_ref=dst, send_sem=misc.at[0], recv_sem=recv,
            device_id=sib, device_id_type=MESH,
        ).wait_recv()

    def isend(k, d):
        dst = (k - d) % 16
        send(ibuf.at[k % 16], ibuf.at[dst], irecv.at[dst], at_z(d))

    def iwait(*ks):
        for k in ks:
            arrived(ibuf.at[k % 16], irecv.at[k % 16])

    def jsend(src, dst, dev):
        send(jbuf.at[src], jbuf.at[dst], jrecv.at[dst], dev)

    def jwait(n):
        arrived(jbuf.at[n], jrecv.at[n])

    def to_sib(n):
        jsend(n, 16 + n, sib)

    def along_q(dp):
        for d in (1, 3, 2):
            jsend(SLOT[dp, 0], SLOT[dp, (4 - d) % 4], at_pq(0, d))

    def prep(n):
        rows = jbuf[n, 384:400, :].astype(F32)
        for h in range(2):
            f = jnp.sum(rows[h * 8:h * 8 + 8, :], axis=0, keepdims=True)
            w = jbuf[n, 256 + h * 64:320 + h * 64, :].astype(F32) * f
            hi = w.astype(BF16)
            lo = (w - hi.astype(F32)).astype(BF16)
            lanes = slice(n * 256 + h * 128, n * 256 + h * 128 + 128)
            vbuf[0:64, lanes] = hi
            vbuf[64:128, lanes] = lo

    hand_over = remote(imsg, ibuf.at[0], irecv.at[0], mirror)
    pl.when(y < 2)(hand_over.start)
    sent.pop()
    sent.append(None)
    for d in (1, 3, 2):
        jsend(0, SLOT[4 - d, 0], at_pq(d, 0))
    along_q(0)
    to_sib(0)
    for d in (3, -3):
        signal(zsem, at_z(d))

    @pl.when(y >= 2)
    def _():
        arrived(ibuf.at[0], irecv.at[0])

    for d in (3, -3, 1, -1, 2, -2):
        isend(0, d)
    prep(0)

    def tile(groups, chunks):
        weights = jnp.concatenate(chunks, axis=1)
        total = None
        for first, n in groups:
            states = jbuf[first:first + n, 0:256, :].reshape(n * 256, 128)
            prod = dot(states, weights)
            square = prod * prod
            local = (square * square).astype(BF16)
            part = dot(vbuf[:, first * 256:(first + n) * 256], local)
            total = part if total is None else total + part
        return total[0:64, :] + total[64:128, :]

    def add_tiles(groups, ks, fresh):
        total = tile(groups, [ibuf[k % 16, 0:128, :] for k in ks])
        for n, k in enumerate(ks):
            part = total[:, n * 128:n * 128 + 128]
            acc[k % 16] = part if fresh else acc[k % 16] + part

    for dp in (1, 3, 2):
        n = SLOT[dp, 0]
        jwait(n)
        along_q(dp)
        to_sib(n)
    for dq in (1, 3):
        n = SLOT[0, dq]
        jwait(n)
        to_sib(n)
    pl.semaphore_wait(zsem, 2)
    for d in (5, -5):
        signal(wsem, at_z(d))
    iwait(-3)
    for d in (3, 1, 2):
        isend(-3, d)
    iwait(3)
    for d in (-3, -1, -2):
        isend(3, d)
    for n in range(16, 21):
        jwait(n)
    iwait(-1, 1, -2, 2)
    for n in list(range(1, 5)) + list(range(16, 21)):
        prep(n)
    wave = [1, -1, 2, -2, 3, -3]
    add_tiles(FIRST, wave, True)

    pl.semaphore_wait(wsem, 2)
    for d in (1, 2, 3):
        signal(xsem, at((x + d) % 4, y, z, core))
    for off in ORDER[6:11]:
        jwait(SLOT[off])
        to_sib(SLOT[off])
    for n in range(21, 27):
        jwait(n)
    for n in list(range(5, 11)) + list(range(21, 27)):
        prep(n)
    add_tiles(SECOND, wave, False)

    pl.semaphore_wait(xsem, 3)
    for d in (1, 2, 3):
        signal(ysem, at(x, (y + d) % 4, z, core))
    iwait(-6)
    isend(-6, 1)
    isend(-6, 2)
    iwait(6)
    isend(6, -1)
    iwait(-4, 4, -5, 5)
    for off in ORDER[11:]:
        jwait(SLOT[off])
        to_sib(SLOT[off])
    add_tiles(FIRST + SECOND, [4, -4, 5, -5, 6, -6], True)

    pl.semaphore_wait(ysem, 3)
    signal(csem, sib)
    iwait(7, -7, 8)
    for n in range(27, 32):
        jwait(n)
    for n in list(range(11, 16)) + list(range(27, 32)):
        prep(n)
    add_tiles(FIRST + SECOND, [0, 7, -7, 8], True)
    pl.semaphore_wait(csem, 1)

    near = ((z - 2 * core - half + 2 + 16) // 4) % 4
    outs = []
    for step, turn in enumerate((2, 1, 3, 0)):
        g = (near + turn) % 4
        h, zs_hi = g // 2, g % 2
        rels = [(8 * zs_hi + 4 * a + 2 * h + b - z + 16) % 16 for a in range(2) for b in range(2)]
        total = tile(THIRD, [ibuf[rel, 0:128, :] for rel in rels])
        for n, rel in enumerate(rels):
            rows = ibuf[rel, 128:144, :].astype(F32)
            scale = jnp.sum(rows, axis=0, keepdims=True) * (INV**4)
            part = acc[rel] + total[:, n * 128:n * 128 + 128]
            m = 4 * step + n
            outbox[m] = (part * scale).astype(BF16)
            dx, dy, dz, dc = 2 * source_y + n // 2, x, 8 * h + 4 * zs_hi + 2 * core + half, n % 2
            mine = (dx == x) & (dy == y) & (dz == z) & (dc == core)
            copy = remote(outbox.at[m], inbox.at[z], rrecv.at[z], at(dx, dy, dz, dc))
            sent.pop()
            sent.append(None)
            pl.when(jnp.logical_not(mine))(copy.start)
            stay = pltpu.make_async_copy(outbox.at[m], inbox.at[z], rrecv.at[z])
            pl.when(mine)(stay.start)
            outs.append((copy, jnp.logical_not(mine)))

    result = None
    for n in range(16):
        arrived(inbox.at[n], rrecv.at[n])
    for n in range(16):
        part = inbox[n].astype(F32)
        result = part if result is None else result + part
    o_ref[...] = result

    for copy in sent:
        if copy is not None:
            copy.wait_send()
    pl.when(y < 2)(hand_over.wait_send)
    for copy, cond in outs:
        pl.when(cond)(copy.wait_send)


def per_device(anomalies, vectors):
    vmem = pl.BlockSpec(memory_space=pltpu.VMEM)
    return pl.pallas_call(
        kernel,
        out_shape=jax.ShapeDtypeStruct((VECS, 128), F32),
        in_specs=[vmem, vmem],
        out_specs=vmem,
        scratch_shapes=[
            pltpu.VMEM((32, JROWS, 128), BF16),
            pltpu.VMEM((128, 8192), BF16),
            pltpu.VMEM((16, IROWS, 128), BF16),
            pltpu.VMEM((IROWS, 128), BF16),
            pltpu.VMEM((16, VECS, 128), F32),
            pltpu.VMEM((16, VECS, 128), BF16),
            pltpu.VMEM((16, VECS, 128), BF16),
            pltpu.SemaphoreType.DMA((64,)),
            pltpu.SemaphoreType.DMA((32,)),
            pltpu.SemaphoreType.DMA((16,)),
            pltpu.SemaphoreType.DMA((16,)),
            pltpu.SemaphoreType.DMA((1,)),
        ] + [pltpu.SemaphoreType.REGULAR] * 5,
        compiler_params=pltpu.CompilerParams(
            collective_id=0, has_side_effects=True, vmem_limit_bytes=48 * 2**20
        ),
    )(anomalies, vectors)


def solution(mesh):
    return jax.shard_map(
        per_device,
        mesh=mesh,
        in_specs=(P(None, ("col", "row")), P(None, ("col", "row"))),
        out_specs=P(None, ("row", "col")),
        check_vma=False,
    )
```

time: 839 us -> 60.8 us (0.07)
  the two profiles are of different devices: /device:TPU:4 before, /device:TPU:39 now
where the time goes in v2:
time: 60.8 us; the launch traced here: 60.6 us
  Pallas kernels  58.4 us (96%)
  local copies, waits for them, and re-layouts  2.21 us (4%)
    pallas_call x1, Pallas kernels, per_device(): pl.pallas_call(kernel, out_shape=jax.ShapeDtypeStruct((VECS, 128), F32),...  58.4 us
    unnamed x5, local copies, waits for them, and re-layouts  2.21 us

profile of v2, /device:TPU:39, one launch (start us, length us, event | category | flops | bytes accessed | tf_op | source)
XLA Modules:
  0.0 60.6 jit_solution(12675602263510687366)
XLA Ops:
  0.0 0.0 copy-start
  0.0 0.8 %copy-done = bf16[128,256]{1,0:T(8,128)(2,1)S(1)} copy-done((bf16[128,256]{1,0:T(8,128)(2,1)S(1)}, bf16[128,256]{1,0:T(8,128)(2,1)}, u32[]{:S(2)}) %copy-start) | copy-done | bytes 65560
  0.8 0.0 copy-start.1
  0.8 0.8 %copy-done.1 = bf16[64,256]{1,0:T(8,128)(2,1)S(1)} copy-done((bf16[64,256]{1,0:T(8,128)(2,1)S(1)}, bf16[64,256]{1,0:T(8,128)(2,1)}, u32[]{:S(2)}) %copy-start.1) | copy-done | bytes 32792
  1.6 58.4 %shard_map.28 = f32[64,128]{1,0:T(8,128)S(1)} custom-call(bf16[128,256]{1,0:T(8,128)(2,1)S(1)} %copy-done, bf16[64,256]{1,0:T(8,128)(2,1)S(1)} %copy-done.1), custom_call_target="tpu_custom_call" | custom-call | tf_op jit(solution)/shard_map/pallas_call | solution.py:295
  60.0 0.6 %copy.4 = f32[64,128]{1,0:T(8,128)} copy(f32[64,128]{1,0:T(8,128)S(1)} %shard_map.28) | data formatting | bytes 65536
Async XLA Ops:
  0.0 0.8 %copy-start = (bf16[128,256]{1,0:T(8,128)(2,1)S(1)}, bf16[128,256]{1,0:T(8,128)(2,1)}, u32[]{:S(2)}) copy-start(bf16[128,256]{1,0:T(8,128)(2,1)} %a_ref.1) | copy-start | bytes 196612
  0.8 0.8 %copy-start.1 = (bf16[64,256]{1,0:T(8,128)(2,1)S(1)}, bf16[64,256]{1,0:T(8,128)(2,1)}, u32[]{:S(2)}) copy-start(bf16[64,256]{1,0:T(8,128)(2,1)} %v_ref.1) | copy-start | bytes 98308

commit v3 on v2

v3 whole, which is shorter than its diff:
```python
import jax
import jax.numpy as jnp
from jax import lax
from jax.experimental import pallas as pl
from jax.experimental.pallas import tpu as pltpu
from jax.sharding import PartitionSpec as P

MESH = pl.DeviceIdType.MESH
F32 = jnp.float32
BF16 = jnp.bfloat16
MEMBERS = 128
VECS = 64
INV = 1.0 / (MEMBERS - 1.0)
JROWS = 400
IROWS = 144
NEAR_Z = (3, -3, 1, -1, 2, -2)

ORDER = [
    (0, 0), (1, 0), (3, 0), (0, 1), (0, 3), (2, 0), (0, 2), (1, 1),
    (1, 3), (3, 1), (3, 3), (1, 2), (3, 2), (2, 1), (2, 3), (2, 2),
]
SLOT = {off: n for n, off in enumerate(ORDER)}
FIRST = [(0, 5), (16, 5)]
REST = [(5, 6), (11, 5), (21, 6), (27, 5)]
TURNS = ((2, 1, 3, 0), (0, 3, 2, 1), (0, 1, 3, 2), (0, 1, 2, 3))


def dot(a, b):
    return jnp.dot(a, b, preferred_element_type=F32)


def split_three(c):
    hi = c.astype(BF16).astype(F32)
    rest = c - hi
    mid = rest.astype(BF16).astype(F32)
    return hi, mid, rest - mid


def kernel(a_hbm, v_hbm, o_ref, a_ref, v_ref, jbuf, vbuf, ibuf, imsg, fto, acc, outbox, inbox,
           send_sem, jrecv, irecv, rrecv, misc, zsem, wsem, xsem, csem):
    loads = [pltpu.make_async_copy(a_hbm, a_ref, misc.at[1]), pltpu.make_async_copy(v_hbm, v_ref, misc.at[2])]
    for copy in loads:
        copy.start()
    row, col = lax.axis_index("row"), lax.axis_index("col")
    x, zh, core = row // 4, (row // 2) % 2, row % 2
    y, zl = col // 8, col % 8
    z = zh * 8 + zl

    def at(x_, y_, z_, core_):
        return {"row": x_ * 4 + (z_ // 8) * 2 + core_, "col": y_ * 8 + z_ % 8}

    p = x + core * (y - x)
    q = y + core * (x - y)

    def at_pq(dp, dq):
        p_, q_ = (p + dp) % 4, (q + dq) % 4
        return at(p_ + core * (q_ - p_), q_ + core * (p_ - q_), z, core)

    def at_z(d, y_=y):
        return at(x, y_, (z + d + 16) % 16, core)

    def signal(sem, dev):
        pl.semaphore_signal(sem, inc=1, device_id=dev, device_id_type=MESH)

    sib = at(x, y, z, 1 - core)

    def same(x_, y_):
        return (x == x_) & (y == y_)

    gives = [(y < 2) & jnp.logical_not(same(2 * y + n, x)) for n in range(2)]
    keeps = [(y < 2) & same(2 * y + n, x) for n in range(2)]
    gets = jnp.logical_not(same(y, x // 2))

    barrier = pltpu.get_barrier_semaphore()
    partners = [sib] + [at_pq(d, 0) for d in (1, 2, 3)] + [at_pq(0, d) for d in (1, 2, 3)]
    partners += [at_z(d) for d in NEAR_Z]
    for dev in partners:
        signal(barrier, dev)

    @pl.when(gets)
    def _():
        signal(barrier, at(y, x // 2, z, core))

    for copy in loads:
        copy.wait()

    wide = a_ref[...].astype(F32)
    spread = jnp.sqrt(jnp.sum(wide * wide, axis=0, keepdims=True) * INV + 1e-06)
    e = jnp.full_like(spread, 2.0**10)
    for k in range(-9, 5):
        e = jnp.where(spread >= 2.0**k, 2.0**-k, e)
    se = spread * e
    factor = 1.0 / (se * se * se * e)
    scaled = wide * e
    narrow = scaled.astype(BF16)
    line = lax.broadcasted_iota(jnp.int32, (16, 128), 0)
    zero = jnp.zeros((16, 128), F32)
    halves = []
    for h in range(2):
        rows = zero
        for n, part in enumerate(split_three(factor[:, h * 128:h * 128 + 128])):
            rows = jnp.where(line == h * 8 + n, part, rows)
        halves.append(rows)

    for n in range(2):
        imsg[n, 0:128] = narrow[:, n * 128:n * 128 + 128]
        imsg[n, 128:144] = halves[n].astype(BF16)

        @pl.when(keeps[n])
        def _():
            ibuf[0] = imsg[n]


    jbuf[0, 0:256, :] = scaled.T.astype(BF16)
    jbuf[0, 256:320, :] = v_ref[:, 0:128]
    jbuf[0, 320:384, :] = v_ref[:, 128:256]
    jbuf[0, 384:400, :] = (halves[0] + halves[1]).astype(BF16)

    pl.semaphore_wait(barrier, len(partners) + sum(g.astype(jnp.int32) for g in gives))

    sent = []

    def remote(src, dst, recv, dev):
        copy = pltpu.make_async_remote_copy(
            src_ref=src, dst_ref=dst, send_sem=send_sem.at[len(sent)], recv_sem=recv,
            device_id=dev, device_id_type=MESH,
        )
        sent.append(copy)
        return copy

    def send(*args):
        remote(*args).start()

    def arrived(dst, recv):
        pltpu.make_async_remote_copy(
            src_ref=dst, dst_ref=dst, send_sem=misc.at[0], recv_sem=recv,
            device_id=sib, device_id_type=MESH,
        ).wait_recv()

    def ichunk(slot):
        return ibuf.at[slot, 0:128]

    def isend(k, d):
        dst = (k - d) % 16
        send(ichunk(k % 16), ichunk(dst), irecv.at[dst], at_z(d))

    def iwait(*ks):
        for k in ks:
            arrived(ichunk(k % 16), irecv.at[k % 16])

    started = []

    def send_if(cond, *args):
        copy = remote(*args)
        sent[-1] = None
        pl.when(cond)(copy.start)
        started.append((copy, cond))

    def jsend(src, dst, dev):
        send(jbuf.at[src], jbuf.at[dst], jrecv.at[dst], dev)

    def jwait(n):
        arrived(jbuf.at[n], jrecv.at[n])

    def to_sib(n):
        jsend(n, 16 + n, sib)

    def along_q(dp):
        for d in (1, 3) if dp % 2 else (1, 3, 2):
            jsend(SLOT[dp, 0], SLOT[dp, 4 - d], at_pq(0, d))

    def across_q(dp):
        jsend(SLOT[dp, 1], SLOT[dp, 2], at_pq(0, 3))

    def prep(n):
        rows = jbuf[n, 384:400, :].astype(F32)
        for h in range(2):
            f = jnp.sum(rows[h * 8:h * 8 + 8, :], axis=0, keepdims=True)
            w = jbuf[n, 256 + h * 64:320 + h * 64, :].astype(F32) * f
            hi = w.astype(BF16)
            lo = (w - hi.astype(F32)).astype(BF16)
            lanes = slice(n * 256 + h * 128, n * 256 + h * 128 + 128)
            vbuf[0:64, lanes] = hi
            vbuf[64:128, lanes] = lo

    for n in range(2):
        send_if(gives[n], imsg.at[n], ibuf.at[0], irecv.at[0], at((2 * y + n) % 4, x, z, core))
    for d in (1, 3, 2):
        jsend(0, SLOT[4 - d, 0], at_pq(d, 0))
    along_q(0)
    to_sib(0)

    @pl.when(gets)
    def _():
        arrived(ibuf.at[0], irecv.at[0])

    for d in NEAR_Z:
        isend(0, d)
    for d in (3, -3):
        signal(zsem, at_z(d))
    prep(0)

    def tile(groups, chunks):
        weights = jnp.concatenate(chunks, axis=1)
        total = None
        for first, n in groups:
            states = jbuf[first:first + n, 0:256, :].reshape(n * 256, 128)
            prod = dot(states, weights)
            square = prod * prod
            local = (square * square).astype(BF16)
            part = dot(vbuf[:, first * 256:(first + n) * 256], local)
            total = part if total is None else total + part
        return total[0:64, :] + total[64:128, :]

    def add_tiles(groups, ks, fresh):
        total = tile(groups, [ibuf[k % 16, 0:128] for k in ks])
        for n, k in enumerate(ks):
            part = total[:, n * 128:n * 128 + 128]
            acc[k % 16] = part if fresh else acc[k % 16] + part

    def take(*offs):
        for off in offs:
            jwait(SLOT[off])
            to_sib(SLOT[off])

    for dp in (1, 3):
        take((dp, 0))
        along_q(dp)
    take((0, 1), (0, 3))
    take((2, 0))
    along_q(2)
    pl.semaphore_wait(zsem, 2)
    for d in (5, -5):
        signal(wsem, at_z(d))
    iwait(-3)
    for d in (3, 1, 2):
        isend(-3, d)
    iwait(3)
    for d in (-3, -1, -2):
        isend(3, d)
    for n in range(1, 5):
        prep(n)
    for n in range(16, 21):
        jwait(n)
        prep(n)
    iwait(-1, 1, -2, 2)
    add_tiles(FIRST, [1, -1, 2, -2, 3, -3], True)

    pl.semaphore_wait(wsem, 2)
    signal(xsem, at(x + 1 - 2 * (x % 2), y, z, core))
    for dp in (1, 3):
        take((dp, 1), (dp, 3))
        across_q(dp)
    take((0, 2))
    for n in range(5, 11):
        prep(n)
    iwait(-6)
    isend(-6, 1)
    isend(-6, 2)
    iwait(6)
    isend(6, -1)
    pl.semaphore_wait(xsem, 1)
    signal(csem, sib)
    for n in range(21, 27):
        jwait(n)
        prep(n)
    iwait(-4, 4, -5, 5)
    add_tiles(FIRST, [4, -4, 5, -5, 6, -6], True)
    take((2, 1), (2, 3))
    take((1, 2), (3, 2), (2, 2))
    for n in range(11, 16):
        prep(n)
    for n in range(27, 32):
        jwait(n)
        prep(n)
    pl.semaphore_wait(csem, 1)

    def deliver(src, dst, recv, zs):
        bit, h = x % 2, (zs // 2) % 2
        dx, dz, dc = x - bit + (zs // 4) % 2, 8 * h + 4 * (zs // 8) + 2 * core + bit, zs % 2
        mine = (dx == x) & (dz == z) & (dc == core)
        send_if(jnp.logical_not(mine), src, dst, recv, at(dx, y, dz, dc))
        pl.when(mine)(pltpu.make_async_copy(src, dst, recv).start)

    deliver(ibuf.at[0, 128:144], fto, misc.at[3], z)

    iwait(7, -7, 8)
    add_tiles(FIRST, [0, 7, -7, 8], True)
    near = ((z - 2 * core - x % 2 + 18) // 4) % 4
    for step in range(4):
        g = sum((near == n).astype(jnp.int32) * turn[step] for n, turn in enumerate(TURNS))
        h, zs_hi = g // 2, g % 2
        begins = [8 * zs_hi + 4 * a + 2 * h + b for a in range(2) for b in range(2)]
        rels = [(zs - z + 16) % 16 for zs in begins]
        total = tile(REST, [ibuf[rel, 0:128] for rel in rels])
        for n, rel in enumerate(rels):
            outbox[4 * step + n] = (acc[rel] + total[:, n * 128:n * 128 + 128]).astype(BF16)
        for n in range(4):
            deliver(outbox.at[4 * step + n], inbox.at[z], rrecv.at[z], begins[n])

    result = None
    arrived(fto, misc.at[3])
    for n in range(16):
        arrived(inbox.at[n], rrecv.at[n])
    for n in range(16):
        part = inbox[n].astype(F32)
        result = part if result is None else result + part
    o_ref[...] = result * (jnp.sum(fto[...].astype(F32), axis=0, keepdims=True) * INV**4)

    for copy in sent:
        if copy is not None:
            copy.wait_send()
    for copy, cond in started:
        pl.when(cond)(copy.wait_send)


def per_device(anomalies, vectors):
    vmem, hbm = pl.BlockSpec(memory_space=pltpu.VMEM), pl.BlockSpec(memory_space=pl.ANY)
    return pl.pallas_call(
        kernel,
        out_shape=jax.ShapeDtypeStruct((VECS, 128), F32),
        in_specs=[hbm, hbm],
        out_specs=vmem,
        scratch_shapes=[
            pltpu.VMEM((MEMBERS, 256), BF16),
            pltpu.VMEM((VECS, 256), BF16),
            pltpu.VMEM((32, JROWS, 128), BF16),
            pltpu.VMEM((128, 8192), BF16),
            pltpu.VMEM((16, IROWS, 128), BF16),
            pltpu.VMEM((2, IROWS, 128), BF16),
            pltpu.VMEM((16, 128), BF16),
            pltpu.VMEM((16, VECS, 128), F32),
            pltpu.VMEM((16, VECS, 128), BF16),
            pltpu.VMEM((16, VECS, 128), BF16),
            pltpu.SemaphoreType.DMA((80,)),
            pltpu.SemaphoreType.DMA((32,)),
            pltpu.SemaphoreType.DMA((16,)),
            pltpu.SemaphoreType.DMA((16,)),
            pltpu.SemaphoreType.DMA((4,)),
        ] + [pltpu.SemaphoreType.REGULAR] * 4,
        compiler_params=pltpu.CompilerParams(
            collective_id=0, has_side_effects=True, vmem_limit_bytes=48 * 2**20
        ),
    )(anomalies, vectors)


def solution(mesh):
    return jax.shard_map(
        per_device,
        mesh=mesh,
        in_specs=(P(None, ("col", "row")), P(None, ("col", "row"))),
        out_specs=P(None, ("row", "col")),
        check_vma=False,
    )
```

time: 60.8 us -> 57 us (0.938)
  the two profiles are of different devices: /device:TPU:39 before, /device:TPU:27 now
where the time goes in v3:
time: 57 us; the launch traced here: 56.8 us
  Pallas kernels  54.5 us (96%)
  local copies, waits for them, and re-layouts  2.21 us (4%)
    pallas_call x1, Pallas kernels, per_device(): pl.pallas_call(kernel, out_shape=jax.ShapeDtypeStruct((VECS, 128), F32),...  54.5 us
    unnamed x5, local copies, waits for them, and re-layouts  2.21 us

profile of v3, /device:TPU:27, one launch (start us, length us, event | category | flops | bytes accessed | tf_op | source)
XLA Modules:
  0.0 56.8 jit_solution(2005565574390994815)
XLA Ops:
  0.0 0.0 copy-start
  0.0 0.8 %copy-done = bf16[128,256]{1,0:T(8,128)(2,1)S(1)} copy-done((bf16[128,256]{1,0:T(8,128)(2,1)S(1)}, bf16[128,256]{1,0:T(8,128)(2,1)}, u32[]{:S(2)}) %copy-start) | copy-done | bytes 65560
  0.8 0.0 copy-start.1
  0.8 0.8 %copy-done.1 = bf16[64,256]{1,0:T(8,128)(2,1)S(1)} copy-done((bf16[64,256]{1,0:T(8,128)(2,1)S(1)}, bf16[64,256]{1,0:T(8,128)(2,1)}, u32[]{:S(2)}) %copy-start.1) | copy-done | bytes 32792
  1.6 54.5 %shard_map.28 = f32[64,128]{1,0:T(8,128)S(1)} custom-call(bf16[128,256]{1,0:T(8,128)(2,1)S(1)} %copy-done, bf16[64,256]{1,0:T(8,128)(2,1)S(1)} %copy-done.1), custom_call_target="tpu_custom_call" | custom-call | tf_op jit(solution)/shard_map/pallas_call | solution.py:319
  56.1 0.6 %copy.4 = f32[64,128]{1,0:T(8,128)} copy(f32[64,128]{1,0:T(8,128)S(1)} %shard_map.28) | data formatting | bytes 65536
Async XLA Ops:
  0.0 0.8 %copy-start = (bf16[128,256]{1,0:T(8,128)(2,1)S(1)}, bf16[128,256]{1,0:T(8,128)(2,1)}, u32[]{:S(2)}) copy-start(bf16[128,256]{1,0:T(8,128)(2,1)} %a_hbm.1) | copy-start | bytes 196612
  0.8 0.8 %copy-start.1 = (bf16[64,256]{1,0:T(8,128)(2,1)S(1)}, bf16[64,256]{1,0:T(8,128)(2,1)}, u32[]{:S(2)}) copy-start(bf16[64,256]{1,0:T(8,128)(2,1)} %v_hbm.1) | copy-start | bytes 98308

commit v4 on v3

--- a/solution.py
+++ b/solution.py
@@ -243,15 +243,15 @@
     for n in range(16, 21):
         jwait(n)
         prep(n)
-    iwait(-1, 1, -2, 2)
-    add_tiles(FIRST, [1, -1, 2, -2, 3, -3], True)
-
-    pl.semaphore_wait(wsem, 2)
-    signal(xsem, at(x + 1 - 2 * (x % 2), y, z, core))
     for dp in (1, 3):
         take((dp, 1), (dp, 3))
         across_q(dp)
+    iwait(-1, 1, -2, 2)
+    add_tiles(FIRST, [1, -1, 2, -2, 3, -3], True)
     take((0, 2))
+
+    pl.semaphore_wait(wsem, 2)
+    signal(xsem, at(x + 1 - 2 * (x % 2), y, z, core))
     for n in range(5, 11):
         prep(n)
     iwait(-6)
@@ -264,10 +264,10 @@
     for n in range(21, 27):
         jwait(n)
         prep(n)
+    take((2, 1), (2, 3))
+    take((1, 2), (3, 2), (2, 2))
     iwait(-4, 4, -5, 5)
     add_tiles(FIRST, [4, -4, 5, -5, 6, -6], True)
-    take((2, 1), (2, 3))
-    take((1, 2), (3, 2), (2, 2))
     for n in range(11, 16):
         prep(n)
     for n in range(27, 32):

time: 57 us -> 55.8 us (0.979)
  the two profiles are of different devices: /device:TPU:27 before, /device:TPU:57 now
where the time goes in v4:
time: 55.8 us; the launch traced here: 55.6 us
  Pallas kernels  53.4 us (96%)
  local copies, waits for them, and re-layouts  2.21 us (4%)
    pallas_call x1, Pallas kernels, per_device(): pl.pallas_call(kernel, out_shape=jax.ShapeDtypeStruct((VECS, 128), F32),...  53.4 us
    unnamed x5, local copies, waits for them, and re-layouts  2.21 us

profile of v4, /device:TPU:57, one launch (start us, length us, event | category | flops | bytes accessed | tf_op | source)
XLA Modules:
  0.0 55.6 jit_solution(7656289283370823607)
XLA Ops:
  0.0 0.0 copy-start
  0.0 0.8 %copy-done = bf16[128,256]{1,0:T(8,128)(2,1)S(1)} copy-done((bf16[128,256]{1,0:T(8,128)(2,1)S(1)}, bf16[128,256]{1,0:T(8,128)(2,1)}, u32[]{:S(2)}) %copy-start) | copy-done | bytes 65560
  0.8 0.0 copy-start.1
  0.8 0.8 %copy-done.1 = bf16[64,256]{1,0:T(8,128)(2,1)S(1)} copy-done((bf16[64,256]{1,0:T(8,128)(2,1)S(1)}, bf16[64,256]{1,0:T(8,128)(2,1)}, u32[]{:S(2)}) %copy-start.1) | copy-done | bytes 32792
  1.6 53.4 %shard_map.28 = f32[64,128]{1,0:T(8,128)S(1)} custom-call(bf16[128,256]{1,0:T(8,128)(2,1)S(1)} %copy-done, bf16[64,256]{1,0:T(8,128)(2,1)S(1)} %copy-done.1), custom_call_target="tpu_custom_call" | custom-call | tf_op jit(solution)/shard_map/pallas_call | solution.py:319
  55.0 0.6 %copy.4 = f32[64,128]{1,0:T(8,128)} copy(f32[64,128]{1,0:T(8,128)S(1)} %shard_map.28) | data formatting | bytes 65536
Async XLA Ops:
  0.0 0.8 %copy-start = (bf16[128,256]{1,0:T(8,128)(2,1)S(1)}, bf16[128,256]{1,0:T(8,128)(2,1)}, u32[]{:S(2)}) copy-start(bf16[128,256]{1,0:T(8,128)(2,1)} %a_hbm.1) | copy-start | bytes 196612
  0.8 0.8 %copy-start.1 = (bf16[64,256]{1,0:T(8,128)(2,1)S(1)}, bf16[64,256]{1,0:T(8,128)(2,1)}, u32[]{:S(2)}) copy-start(bf16[64,256]{1,0:T(8,128)(2,1)} %v_hbm.1) | copy-start | bytes 98308

commit v5 on v4

--- a/solution.py
+++ b/solution.py
@@ -247,7 +247,7 @@
         take((dp, 1), (dp, 3))
         across_q(dp)
     iwait(-1, 1, -2, 2)
-    add_tiles(FIRST, [1, -1, 2, -2, 3, -3], True)
+    add_tiles(FIRST, [0, 1, -1, 2, -2, 3, -3], True)
     take((0, 2))
 
     pl.semaphore_wait(wsem, 2)
@@ -255,8 +255,8 @@
     for n in range(5, 11):
         prep(n)
     iwait(-6)
+    isend(-6, 2)
     isend(-6, 1)
-    isend(-6, 2)
     iwait(6)
     isend(6, -1)
     pl.semaphore_wait(xsem, 1)
@@ -285,7 +285,7 @@
     deliver(ibuf.at[0, 128:144], fto, misc.at[3], z)
 
     iwait(7, -7, 8)
-    add_tiles(FIRST, [0, 7, -7, 8], True)
+    add_tiles(FIRST, [7, -7, 8], True)
     near = ((z - 2 * core - x % 2 + 18) // 4) % 4
     for step in range(4):
         g = sum((near == n).astype(jnp.int32) * turn[step] for n, turn in enumerate(TURNS))

time: 55.8 us -> 55.5 us (level)
  no operation moved by 1% of the time
where the time goes in v5:
time: 55.5 us; the launch traced here: 55.3 us
  Pallas kernels  53.1 us (96%)
  local copies, waits for them, and re-layouts  2.21 us (4%)
    pallas_call x1, Pallas kernels, per_device(): pl.pallas_call(kernel, out_shape=jax.ShapeDtypeStruct((VECS, 128), F32),...  53.1 us
    unnamed x5, local copies, waits for them, and re-layouts  2.21 us

profile of v5, /device:TPU:57, one launch (start us, length us, event | category | flops | bytes accessed | tf_op | source)
XLA Modules:
  0.0 55.3 jit_solution(11278868929010620735)
XLA Ops:
  0.0 0.0 copy-start
  0.0 0.8 %copy-done = bf16[128,256]{1,0:T(8,128)(2,1)S(1)} copy-done((bf16[128,256]{1,0:T(8,128)(2,1)S(1)}, bf16[128,256]{1,0:T(8,128)(2,1)}, u32[]{:S(2)}) %copy-start) | copy-done | bytes 65560
  0.8 0.0 copy-start.1
  0.8 0.8 %copy-done.1 = bf16[64,256]{1,0:T(8,128)(2,1)S(1)} copy-done((bf16[64,256]{1,0:T(8,128)(2,1)S(1)}, bf16[64,256]{1,0:T(8,128)(2,1)}, u32[]{:S(2)}) %copy-start.1) | copy-done | bytes 32792
  1.6 53.1 %shard_map.28 = f32[64,128]{1,0:T(8,128)S(1)} custom-call(bf16[128,256]{1,0:T(8,128)(2,1)S(1)} %copy-done, bf16[64,256]{1,0:T(8,128)(2,1)S(1)} %copy-done.1), custom_call_target="tpu_custom_call" | custom-call | tf_op jit(solution)/shard_map/pallas_call | solution.py:319
  54.7 0.6 %copy.4 = f32[64,128]{1,0:T(8,128)} copy(f32[64,128]{1,0:T(8,128)S(1)} %shard_map.28) | data formatting | bytes 65536
Async XLA Ops:
  0.0 0.8 %copy-start = (bf16[128,256]{1,0:T(8,128)(2,1)S(1)}, bf16[128,256]{1,0:T(8,128)(2,1)}, u32[]{:S(2)}) copy-start(bf16[128,256]{1,0:T(8,128)(2,1)} %a_hbm.1) | copy-start | bytes 196612
  0.8 0.8 %copy-start.1 = (bf16[64,256]{1,0:T(8,128)(2,1)S(1)}, bf16[64,256]{1,0:T(8,128)(2,1)}, u32[]{:S(2)}) copy-start(bf16[64,256]{1,0:T(8,128)(2,1)} %v_hbm.1) | copy-start | bytes 98308
